TPU v7x, 32 devices: a whole 2x2x4 slice. The times are simulated.
32 devices in a mesh: group: 2 (over x), blk: 8 (over z, y), uly: 2 (over core).
Axes of the slice: x: 2, y: 2, z: 4, core: 2. Of those that a mesh axis runs over, the one named last changes fastest.
Arguments:
- queries: bfloat16 [4096, 4096], P(('group', 'blk', 'uly')), parts along dimension 0, may hold values from -6 to 6
- key_states: bfloat16 [4096, 1024], P(('group', 'blk', 'uly')), parts along dimension 0, may hold values from -6 to 6
- value_states: bfloat16 [4096, 1024], P(('group', 'blk', 'uly')), parts along dimension 0, may hold values from -6 to 6
- out_grad: bfloat16 [4096, 4096], P(('group', 'blk', 'uly')), parts along dimension 0, may hold values from -6 to 6
- pattern: int32 [32, 8], replicated, may hold values from 0 to 31, as said below
Outputs:
- attended: bfloat16 [4096, 4096], P(('group', 'blk', 'uly')), parts along dimension 0
- query_grad: bfloat16 [4096, 4096], P(('group', 'blk', 'uly')), parts along dimension 0
- key_grad: bfloat16 [4096, 1024], P(('group', 'blk', 'uly')), parts along dimension 0
- value_grad: bfloat16 [4096, 1024], P(('group', 'blk', 'uly')), parts along dimension 0
There are 2 independent parts, one for each index of `group`. A program takes and returns all parts, laid end to end along the dimension named above; an argument that names none is the same for every part. Nothing has to cross between parts.
Inputs may be any that keep to these rules, and one draw needn't show every extreme that they name: `pattern`: columns 0 to 2 of row i are i - 1, i, i + 1 modulo 32; columns 3 and 4 are 0 and 31; the last 3 columns are random blocks. Take the rows s * 4 to (s + 1) * 4 - 1 of one group s and count each listed block once: the blocks of any other group r (blocks r * 4 to (r + 1) * 4 - 1) number at most 2, and exactly 2 for some other group of every group.
All inputs are finite; a program needn't handle non-finite values.
Results may differ from a plain program's by a relative error of at most 0.024.
Values may be sent and summed in bfloat16 or wider, within the bound.
A program may use at most 128 MiB of HBM per device.

v0:
```python
import functools
import math

import jax
import jax.numpy as jnp
from jax import lax
from jax.experimental import pallas as pl
from jax.experimental.pallas import tpu as pltpu
from jax.sharding import PartitionSpec as P

HD = 128
BLOCK = 64
CAP = 2


def dot(a, b, dims):
    return lax.dot_general(a, b, (dims, ((), ())), preferred_element_type=jnp.float32)


def attend(
    repeat, qb, kb, rows_ref, pool_ref, q_ref, do_ref, k_ref, v_ref,
    att_ref, dq_ref, grad_ref, kl, vl, acc_k, acc_v,
):
    scale = HD ** (-0.5)
    acc_k[...] = jnp.zeros_like(acc_k)
    acc_v[...] = jnp.zeros_like(acc_v)
    for i in range(qb):
        tokens = pl.ds(i * BLOCK, BLOCK)
        for c in range(kb):
            row = pl.multiple_of(rows_ref[i * kb + c] * BLOCK, BLOCK)
            kl[pl.ds(c * BLOCK, BLOCK), :] = k_ref[pl.ds(row, BLOCK), :]
            vl[pl.ds(c * BLOCK, BLOCK), :] = v_ref[pl.ds(row, BLOCK), :]
        q = jnp.concatenate([q_ref[tokens, r * HD:(r + 1) * HD] for r in range(repeat)], axis=0)
        do = jnp.concatenate([do_ref[tokens, r * HD:(r + 1) * HD] for r in range(repeat)], axis=0)
        k = kl[...]
        v = vl[...]
        s = dot(k, q, ((1,), (1,))) * (scale * math.log2(math.e))
        e = jnp.exp2(s - jnp.max(s, axis=0, keepdims=True))
        p = e * (1.0 / jnp.sum(e, axis=0, keepdims=True))
        p_low = p.astype(jnp.bfloat16)
        att = dot(v, p_low, ((0,), (0,))).astype(jnp.bfloat16)
        do_t = jnp.transpose(do.astype(jnp.float32))
        delta = jnp.sum(do_t * att.astype(jnp.float32), axis=0, keepdims=True)
        dp = dot(v, do, ((1,), (1,)))
        ds_low = (p * (dp - delta)).astype(jnp.bfloat16)
        dq = dot(k, ds_low, ((0,), (0,))) * scale
        dk = dot(ds_low, q, ((1,), (0,))) * scale
        dv = dot(p_low, do, ((1,), (0,)))
        att_n = jnp.transpose(att.astype(jnp.float32)).astype(jnp.bfloat16)
        dq_n = jnp.transpose(dq).astype(jnp.bfloat16)
        for r in range(repeat):
            att_ref[tokens, r * HD:(r + 1) * HD] = att_n[r * BLOCK:(r + 1) * BLOCK]
            dq_ref[tokens, r * HD:(r + 1) * HD] = dq_n[r * BLOCK:(r + 1) * BLOCK]
        for c in range(kb):
            at = pl.ds(pl.multiple_of(pool_ref[i * kb + c] * BLOCK, BLOCK), BLOCK)
            acc_k[at, :] += dk[c * BLOCK:(c + 1) * BLOCK]
            acc_v[at, :] += dv[c * BLOCK:(c + 1) * BLOCK]
    grad_ref[0] = acc_k[...].astype(jnp.bfloat16)
    grad_ref[1] = acc_v[...].astype(jnp.bfloat16)


def attend_call(rows, pool, q, do, kv, qb, kb, pool_size):
    tokens, width = q.shape
    kv_rows, kv2 = kv.shape
    groups = kv2 // 2 // HD
    cols = width // groups
    q_spec = pl.BlockSpec((tokens, cols), lambda g, *_: (0, g))
    pr = pool_size * BLOCK
    return pl.pallas_call(
        functools.partial(attend, cols // HD, qb, kb),
        out_shape=(
            jax.ShapeDtypeStruct((tokens, width), jnp.bfloat16),
            jax.ShapeDtypeStruct((tokens, width), jnp.bfloat16),
            jax.ShapeDtypeStruct((2, pr, kv2 // 2), jnp.bfloat16),
        ),
        grid_spec=pltpu.PrefetchScalarGridSpec(
            num_scalar_prefetch=2,
            grid=(groups,),
            in_specs=[
                q_spec,
                q_spec,
                pl.BlockSpec((kv_rows, HD), lambda g, *_: (0, g)),
                pl.BlockSpec((kv_rows, HD), lambda g, *_: (0, groups + g)),
            ],
            out_specs=[q_spec, q_spec, pl.BlockSpec((2, pr, HD), lambda g, *_: (0, 0, g))],
            scratch_shapes=[
                pltpu.VMEM((kb * BLOCK, HD), jnp.bfloat16),
                pltpu.VMEM((kb * BLOCK, HD), jnp.bfloat16),
                pltpu.VMEM((pr, HD), jnp.float32),
                pltpu.VMEM((pr, HD), jnp.float32),
            ],
        ),
        compiler_params=pltpu.CompilerParams(vmem_limit_bytes=40 * 1024 * 1024),
        name="attend",
    )(rows, pool, q, do, kv, kv)


def combine(shards, qb, asked_ref, rank_ref, own_ref, back_ref, out_ref):
    for l in range(qb):
        out_rows = pl.ds(l * BLOCK, BLOCK)
        total = own_ref[0, out_rows, :].astype(jnp.float32)
        for d in range(shards):
            row = pl.multiple_of(rank_ref[d * qb + l] * BLOCK, BLOCK)
            term = back_ref[d, 0, pl.ds(row, BLOCK), :].astype(jnp.float32)
            total = total + jnp.where(asked_ref[d * qb + l] > 0, term, 0.0)
        out_ref[0, out_rows, :] = total.astype(jnp.bfloat16)


def combine_call(asked, rank, grads, back, qb):
    shards = back.shape[0]
    width = back.shape[-1]
    return pl.pallas_call(
        functools.partial(combine, shards, qb),
        out_shape=jax.ShapeDtypeStruct((2, qb * BLOCK, width), jnp.bfloat16),
        grid_spec=pltpu.PrefetchScalarGridSpec(
            num_scalar_prefetch=2,
            grid=(2,),
            in_specs=[
                pl.BlockSpec((1, qb * BLOCK, width), lambda t, *_: (t, 0, 0)),
                pl.BlockSpec((shards, 1, CAP * BLOCK, width), lambda t, *_: (0, t, 0, 0)),
            ],
            out_specs=pl.BlockSpec((1, qb * BLOCK, width), lambda t, *_: (t, 0, 0)),
        ),
        compiler_params=pltpu.CompilerParams(vmem_limit_bytes=40 * 1024 * 1024),
        name="combine",
    )(asked, rank, grads, back)


def plan(pattern, position, shards, qb):
    blocks, kb = pattern.shape
    ids = jnp.arange(blocks, dtype=jnp.int32)
    owner = ids // qb
    per_shard = pattern.reshape(shards, qb * kb)
    listed = jnp.any(per_shard[:, :, None] == ids[None, None, :], axis=1).astype(jnp.int32)
    before = ((owner[:, None] == owner[None, :]) & (ids[:, None] < ids[None, :])).astype(jnp.int32)
    rank_all = jnp.sum(listed[:, :, None] * before[None], axis=1)
    mine = lax.dynamic_slice_in_dim(per_shard, position, 1, 0).reshape(-1)
    my_rank = lax.dynamic_slice_in_dim(rank_all, position, 1, 0)
    rank = jnp.sum(jnp.where(mine[:, None] == ids[None, :], my_rank, 0), axis=1)
    pool = jnp.where(mine // qb == position, mine % qb, qb + (mine // qb) * CAP + rank)
    others = jnp.arange(shards, dtype=jnp.int32)[:, None] != position
    asked = lax.dynamic_slice_in_dim(listed, position * qb, qb, 1) * others
    asked_rank = jnp.where(asked > 0, lax.dynamic_slice_in_dim(rank_all, position * qb, qb, 1), 0)
    return mine, pool, asked.reshape(-1), asked_rank.reshape(-1)


def on_device(queries, key_states, value_states, out_grad, pattern):
    shards = lax.axis_size("blk")
    position = lax.axis_index("blk")
    swap = functools.partial(lax.all_to_all, axis_name="uly", split_axis=1, concat_axis=0, tiled=True)
    unswap = functools.partial(lax.all_to_all, axis_name="uly", split_axis=0, concat_axis=1, tiled=True)
    k, v = swap(key_states), swap(value_states)
    everything = lax.all_gather(jnp.concatenate([k, v], axis=1), "blk", axis=0, tiled=True)
    q, do = swap(queries), swap(out_grad)
    qb = q.shape[0] // BLOCK
    kb = pattern.shape[1]
    rows, pool, asked, rank = plan(pattern, position, shards, qb)
    att, dq, grads = attend_call(rows, pool, q, do, everything, qb, kb, qb + shards * CAP)
    width = grads.shape[-1]
    sent = grads[:, qb * BLOCK:].reshape(2, shards, CAP * BLOCK, width).transpose(1, 0, 2, 3)
    back = lax.all_to_all(sent, "blk", split_axis=0, concat_axis=0, tiled=True)
    kv_grad = combine_call(asked, rank, grads, back, qb)
    return unswap(att), unswap(dq), unswap(kv_grad[0]), unswap(kv_grad[1])


def solution(mesh):
    split = P(("group", "blk", "uly"), None)
    return jax.shard_map(
        on_device,
        mesh=mesh,
        in_specs=(split, split, split, split, P()),
        out_specs=(split, split, split, split),
        check_vma=False,
    )
```

profile of v0, /device:TPU:0, one launch (start us, length us, event | category | flops | bytes accessed | tf_op | source)
XLA Modules:
  0.0 205.5 jit_solution(16699502466168466191)
XLA Ops:
  7.2 0.0 copy-start.7
  7.2 1.8 copy.54
  8.9 3.4 %all-to-all-start.2 = ((bf16[128,2,512]{2,0,1:T(8,128)(2,1)}), bf16[128,2,512]{2,0,1:T(8,128)(2,1)S(1)}, u32[]{:S(2)}, u32[]{:S(2)}) async-start(bf16[128,2,512]{2,0,1:T(8,128)(2,1)} %bitcast.53), calls=%async_computation.2 | async-start | bytes 524288 | tf_op jit(solution)/shard_map/all_to_all | solution.py:152
  12.4 0.0 all-gather.2.cloned.1.call-start
  12.4 1.0 copy.53
  13.4 0.5 all-to-all-done.2
  13.9 3.9 %all_to_all.157 = bf16[128,2,512]{2,0,1:T(8,128)(2,1)S(1)} all-to-all(bf16[128,2,512]{2,0,1:T(8,128)(2,1)S(1)} %bitcast.66), channel_id=1, replica_groups=mesh['group'=2,'blk'=8,'uly'=2] {'uly'}, dimensions={1} | all-to-all | bytes 524288 | tf_op jit(solution)/shard_map/all_to_all | solution.py:152
  17.9 0.9 pad_maximum_fusion
  18.7 0.0 all-gather.2.cloned.1.call-update
  18.7 0.0 copy-done.7
  18.8 0.0 copy-start.9
  18.8 0.0 copy-start.8
  18.8 1.0 copy.52
  19.8 3.6 %all-to-all-start = ((bf16[128,2,2048]{2,0,1:T(8,128)(2,1)}), bf16[128,2,2048]{2,0,1:T(8,128)(2,1)S(1)}, u32[]{:S(2)}, u32[]{:S(2)}) async-start(bf16[128,2,2048]{2,0,1:T(8,128)(2,1)} %bitcast.51), calls=%async_computation | async-start | bytes 2097152 | tf_op jit(solution)/shard_map/all_to_all | solution.py:154
  23.4 0.0 copy-done.9
  23.4 0.1 copy.27
  23.5 0.1 reshape.128
  23.6 0.1 fusion
  23.7 0.0 copy-done.8
  23.7 0.1 copy.51
  23.8 0.1 fusion.2
  23.9 0.1 multiply_reduce_fusion
  24.1 0.2 select_reduce_fusion
  24.3 1.2 all-to-all-done
  25.5 0.0 copy-start.1
  25.5 5.4 %all_to_all.158 = bf16[128,2,2048]{2,0,1:T(8,128)(2,1)} all-to-all(bf16[128,2,2048]{2,0,1:T(8,128)(2,1)S(1)} %bitcast.61), channel_id=1, replica_groups=mesh['group'=2,'blk'=8,'uly'=2] {'uly'}, dimensions={1} | all-to-all | bytes 2097152 | tf_op jit(solution)/shard_map/all_to_all | solution.py:154
  30.9 64.1 %all-gather.2.cloned.1.call-done.k_ref.v_ref = bf16[2048,1024]{1,0:T(8,128)(2,1)} async-done(((bf16[256,1024]{1,0:T(8,128)(2,1)}), bf16[2048,1024]{1,0:T(8,128)(2,1)}) %all-gather.2.cloned.1.call-update) | async-done | bytes 4194320 | tf_op jit(solution)/shard_map/all_gather | solution.py:153
  95.0 0.0 copy-done.1
  95.0 0.0 copy-start
  95.0 2.2 %copy-done = bf16[2048,1024]{1,0:T(8,128)(2,1)S(1)} copy-done((bf16[2048,1024]{1,0:T(8,128)(2,1)S(1)}, bf16[2048,1024]{1,0:T(8,128)(2,1)}, u32[]{:S(2)}) %copy-start) | copy-done | bytes 4194328
  97.2 0.0 copy-start.2
  97.2 1.2 copy-done.2
  98.4 0.0 copy-start.3
  98.4 1.2 copy-done.3
  99.6 18.5 %attend.1 = (bf16[256,2048]{1,0:T(8,128)(2,1)S(1)}, bf16[256,2048]{1,0:T(8,128)(2,1)S(1)}, bf16[2,1280,512]{2,1,0:T(8,128)(2,1)S(1)}) custom-call(s32[32]{0:T(128)S(1)} %fusion.3.rows_ref, s32[32]{0:T(128)S(1)} %compare_select_fusion.pool_ref, bf16[256,2048]{1,0:T(8,128)(2,1)S(1)} %bitcast.54, bf16[256,2048]{1,0:T(8,128)(2,1)S(1)} %bitcast.55, ...), custom_call_target="tpu_custom_call" | custom-call | tf_op jit(solution)/shard_map/attend/pallas_call | solution.py:69
  118.2 0.0 copy-start.4
  118.2 1.0 copy-done.4
  119.2 0.0 copy-start.5
  119.2 1.0 copy-done.5
  120.1 4.4 %all-to-all-start.5 = ((bf16[2,128,2048]{2,1,0:T(8,128)(2,1)}), bf16[2,128,2048]{2,1,0:T(8,128)(2,1)}, u32[]{:S(2)}, u32[]{:S(2)}) async-start(bf16[2,128,2048]{2,1,0:T(8,128)(2,1)} %bitcast.57), calls=%async_computation.5 | async-start | bytes 2097152 | tf_op jit(solution)/shard_map/all_to_all | solution.py:163
  124.5 0.1 slice.9
  124.7 1.5 copy.50
  126.2 0.5 all-to-all-done.5
  126.8 6.6 %all_to_all.159 = bf16[2,128,2048]{2,1,0:T(8,128)(2,1)} all-to-all(bf16[2,128,2048]{2,1,0:T(8,128)(2,1)} %bitcast.56), channel_id=1, replica_groups=mesh['group'=2,'blk'=8,'uly'=2] {'uly'}, dimensions={0} | all-to-all | bytes 2097152 | tf_op jit(solution)/shard_map/all_to_all | solution.py:163
  133.4 4.3 %all-to-all-start.6 = ((bf16[8,2,128,512]{3,2,1,0:T(8,128)(2,1)}), bf16[8,2,128,512]{3,2,1,0:T(8,128)(2,1)}, u32[]{:S(2)}, u32[]{:S(2)}) async-start(bf16[8,2,128,512]{3,2,1,0:T(8,128)(2,1)} %bitcast.58), calls=%async_computation.6 | async-start | bytes 4194304 | tf_op jit(solution)/shard_map/all_to_all | solution.py:161
  137.8 0.1 dynamic-slice_select_fusion
  137.8 0.1 reshape.131.rank_ref
  137.9 0.1 reshape.130.asked_ref
  138.0 0.0 copy-start.6
  138.0 2.4 %copy.42 = bf16[2,16,8,2048]{3,2,0,1:T(8,128)(2,1)} copy(bf16[2,16,8,2048]{3,2,1,0:T(8,128)(2,1)} %bitcast.34) | data formatting | bytes 2097152 | tf_op jit(solution)/shard_map/all_to_all | solution.py:163
  140.4 0.0 copy-done.6
  140.4 1.0 copy.41
  141.4 45.1 %all-to-all-done.6.back_ref = bf16[8,2,128,512]{3,2,1,0:T(8,128)(2,1)} async-done(((bf16[8,2,128,512]{3,2,1,0:T(8,128)(2,1)}), bf16[8,2,128,512]{3,2,1,0:T(8,128)(2,1)}, u32[]{:S(2)}, u32[]{:S(2)}) %all-to-all-start.6) | async-done | bytes 2097184 | tf_op jit(solution)/shard_map/all_to_all | solution.py:161
  186.6 2.7 %combine.1 = bf16[2,256,512]{2,1,0:T(8,128)(2,1)S(1)} custom-call(s32[32]{0:T(128)S(1)} %reshape.130.asked_ref, s32[32]{0:T(128)S(1)} %reshape.131.rank_ref, bf16[2,1280,512]{2,1,0:T(8,128)(2,1)S(1)} %get-tuple-element.9.own_ref, bf16[8,2,128,512]{3,2,1,0:T(8,128)(2,1)} %all-to-all-done.6.back_ref), custom_call_target="tpu_custom_call" | custom-call | tf_op jit(solution)/shard_map/combine/pallas_call | solution.py:112
  189.3 3.9 %all_to_all.160 = bf16[2,128,512]{2,1,0:T(8,128)(2,1)S(1)} all-to-all(bf16[2,128,512]{2,1,0:T(8,128)(2,1)S(1)} %bitcast.71), channel_id=1, replica_groups=mesh['group'=2,'blk'=8,'uly'=2] {'uly'}, dimensions={0} | all-to-all | bytes 524288 | tf_op jit(solution)/shard_map/all_to_all | solution.py:163
  193.3 0.7 copy.43
  194.0 3.9 %all_to_all.161 = bf16[2,128,512]{2,1,0:T(8,128)(2,1)S(1)} all-to-all(bf16[2,128,512]{2,1,0:T(8,128)(2,1)S(1)} %bitcast.70), channel_id=1, replica_groups=mesh['group'=2,'blk'=8,'uly'=2] {'uly'}, dimensions={0} | all-to-all | bytes 524288 | tf_op jit(solution)/shard_map/all_to_all | solution.py:163
  197.9 0.7 copy.44
  (7 shorter events, 0.1 us)
Async XLA Ops:
  7.2 11.6 %copy-start.7 = (bf16[128,4096]{1,0:T(8,128)(2,1)S(1)}, bf16[128,4096]{1,0:T(8,128)(2,1)}, u32[]{:S(2)}) copy-start(bf16[128,4096]{1,0:T(8,128)(2,1)} %param.5) | copy-start | bytes 3145732
  8.9 5.0 %all-to-all-start.2 = ((bf16[128,2,512]{2,0,1:T(8,128)(2,1)}), bf16[128,2,512]{2,0,1:T(8,128)(2,1)S(1)}, u32[]{:S(2)}, u32[]{:S(2)}) async-start(bf16[128,2,512]{2,0,1:T(8,128)(2,1)} %bitcast.53), calls=%async_computation.2 | async-start | bytes 524288 | tf_op jit(solution)/shard_map/all_to_all | solution.py:152
  12.4 82.6 %all-gather.2.cloned.1.call-start = ((), (), s32[]{:S(2)}) async-start(), calls=%async_computation.9 | async-start | bytes 4718592 | tf_op jit(solution)/shard_map/all_gather | solution.py:153
  18.8 4.7 %copy-start.9 = (s32[32,8]{0,1:T(8,128)S(1)}, s32[32,8]{0,1:T(8,128)}, u32[]{:S(2)}) copy-start(s32[32,8]{0,1:T(8,128)} %param.9) | copy-start | bytes 3076
  18.8 4.9 %copy-start.8 = (bf16[128,4096]{1,0:T(8,128)(2,1)S(1)}, bf16[128,4096]{1,0:T(8,128)(2,1)}, u32[]{:S(2)}) copy-start(bf16[128,4096]{1,0:T(8,128)(2,1)} %param.8) | copy-start | bytes 3145732
  19.8 5.7 %all-to-all-start = ((bf16[128,2,2048]{2,0,1:T(8,128)(2,1)}), bf16[128,2,2048]{2,0,1:T(8,128)(2,1)S(1)}, u32[]{:S(2)}, u32[]{:S(2)}) async-start(bf16[128,2,2048]{2,0,1:T(8,128)(2,1)} %bitcast.51), calls=%async_computation | async-start | bytes 2097152 | tf_op jit(solution)/shard_map/all_to_all | solution.py:154
  25.5 69.5 %copy-start.1 = (bf16[128,2,2048]{2,0,1:T(8,128)(2,1)}, bf16[128,2,2048]{2,0,1:T(8,128)(2,1)S(1)}, u32[]{:S(2)}) copy-start(bf16[128,2,2048]{2,0,1:T(8,128)(2,1)S(1)} %all-to-all-done) | copy-start | bytes 3145732
  95.0 2.2 %copy-start = (bf16[2048,1024]{1,0:T(8,128)(2,1)S(1)}, bf16[2048,1024]{1,0:T(8,128)(2,1)}, u32[]{:S(2)}) copy-start(bf16[2048,1024]{1,0:T(8,128)(2,1)} %all-gather.2.cloned.1.call-done.k_ref.v_ref) | copy-start | bytes 12582916
  97.2 1.2 copy-start.2
  98.4 1.2 copy-start.3
  118.2 1.0 copy-start.4
  119.2 1.0 copy-start.5
  120.1 6.7 %all-to-all-start.5 = ((bf16[2,128,2048]{2,1,0:T(8,128)(2,1)}), bf16[2,128,2048]{2,1,0:T(8,128)(2,1)}, u32[]{:S(2)}, u32[]{:S(2)}) async-start(bf16[2,128,2048]{2,1,0:T(8,128)(2,1)} %bitcast.57), calls=%async_computation.5 | async-start | bytes 2097152 | tf_op jit(solution)/shard_map/all_to_all | solution.py:163
  133.4 53.2 %all-to-all-start.6 = ((bf16[8,2,128,512]{3,2,1,0:T(8,128)(2,1)}), bf16[8,2,128,512]{3,2,1,0:T(8,128)(2,1)}, u32[]{:S(2)}, u32[]{:S(2)}) async-start(bf16[8,2,128,512]{3,2,1,0:T(8,128)(2,1)} %bitcast.58), calls=%async_computation.6 | async-start | bytes 4194304 | tf_op jit(solution)/shard_map/all_to_all | solution.py:161
  138.0 2.4 %copy-start.6 = (bf16[2,128,2048]{2,1,0:T(8,128)(2,1)S(1)}, bf16[2,128,2048]{2,1,0:T(8,128)(2,1)}, u32[]{:S(2)}) copy-start(bf16[2,128,2048]{2,1,0:T(8,128)(2,1)} %all_to_all.159) | copy-start | bytes 3145732
Sparse Core Ops, SparseCore 0:
  18.9 76.0 all-gather.1
where the time goes:
time: 206 us; the launch traced here: 205 us
  waiting for transfers between devices  112 us (54%)
  blocking collectives  23.8 us (12%)
  Pallas kernels  21.2 us (10%)
  local copies, waits for them, and re-layouts  17.4 us (8%)
  starting transfers between devices  15.8 us (8%)
  between operations  14.2 us (7%)
    all_gather x1, waiting for transfers between devices, on_device(): lax.all_gather(jnp.concatenate([k, v], axis=1), 'blk', axis=0, tiled=True)  64.1 us
    all_to_all x1, waiting for transfers between devices, on_device(): back = lax.all_to_all(sent, 'blk', split_axis=0, concat_axis=0, tiled=True)  45.1 us
    pallas_call x1, Pallas kernels, attend_call(): pl.pallas_call(functools.partial(attend, cols // HD, qb, kb), out_shape=(...  18.5 us
    all_to_all x3, blocking collectives, on_device(): return (unswap(att), unswap(dq), unswap(kv_grad[0]), unswap(kv_grad[1]))  14.5 us
    unnamed x21, local copies, waits for them, and re-layouts  6.67 us
    all_to_all x1, blocking collectives, on_device(): q, do = (swap(queries), swap(out_grad))  5.36 us
    all_to_all x4, local copies, waits for them, and re-layouts, on_device(): return (unswap(att), unswap(dq), unswap(kv_grad[0]), unswap(kv_grad[1]))  4.9 us
    all_to_all x1, starting transfers between devices, on_device(): return (unswap(att), unswap(dq), unswap(kv_grad[0]), unswap(kv_grad[1]))  4.41 us
  transfers between devices with their start and end apart: 5, of which 5 were waited for; matrix products, arithmetic and copies ran while one was open for 4% of the time, Pallas kernels for 0%

commit v1 on v0

--- a/solution.py
+++ b/solution.py
@@ -95,35 +95,226 @@
     )(rows, pool, q, do, kv, kv)
 
 
-def combine(shards, qb, asked_ref, rank_ref, own_ref, back_ref, out_ref):
-    for l in range(qb):
-        out_rows = pl.ds(l * BLOCK, BLOCK)
-        total = own_ref[0, out_rows, :].astype(jnp.float32)
-        for d in range(shards):
-            row = pl.multiple_of(rank_ref[d * qb + l] * BLOCK, BLOCK)
-            term = back_ref[d, 0, pl.ds(row, BLOCK), :].astype(jnp.float32)
-            total = total + jnp.where(asked_ref[d * qb + l] > 0, term, 0.0)
-        out_ref[0, out_rows, :] = total.astype(jnp.bfloat16)
-
-
-def combine_call(asked, rank, grads, back, qb):
-    shards = back.shape[0]
-    width = back.shape[-1]
+MESH = pl.DeviceIdType.MESH
+ANY = pl.BlockSpec(memory_space=pl.ANY)
+SMEM = pl.BlockSpec(memory_space=pltpu.SMEM)
+
+
+def part(index, size):
+    return pl.ds(pl.multiple_of(index * size, size), size)
+
+
+def greet(shards, me, mate):
+    barrier = pltpu.get_barrier_semaphore()
+    pl.semaphore_signal(barrier, inc=1, device_id={"uly": mate}, device_id_type=MESH)
+
+    def one(o, carry):
+        pl.semaphore_signal(
+            barrier, inc=1, device_id={"blk": lax.rem(me + o, shards)}, device_id_type=MESH
+        )
+        return carry
+
+    lax.fori_loop(1, shards, one, 0)
+    pl.semaphore_wait(barrier, shards)
+
+
+def to_mate(src, dst, sems, at, mate):
+    return pltpu.make_async_remote_copy(
+        src_ref=src, dst_ref=dst, send_sem=sems.at[0, at], recv_sem=sems.at[1, at],
+        device_id={"uly": mate}, device_id_type=MESH,
+    )
+
+
+def bring(
+    shards, qb, idx_ref, q_ref, do_ref, k_ref, v_ref, qh_ref, doh_ref, pool_ref,
+    kv, out, local, mate_sems, blk_sems,
+):
+    me = lax.axis_index("blk")
+    core = lax.axis_index("uly")
+    mate = 1 - core
+    rows, width = q_ref.shape
+    half, kv_half = width // 2, k_ref.shape[1] // 2
+    here = part(core, rows)
+    first = pl.ds(0, kv_half)
+    second = pl.ds(kv_half, kv_half)
+    greet(shards, me, mate)
+    ks = to_mate(k_ref.at[:, part(mate, kv_half)], kv.at[here, first], mate_sems, 0, mate)
+    vs = to_mate(v_ref.at[:, part(mate, kv_half)], kv.at[here, second], mate_sems, 1, mate)
+    ks.start()
+    vs.start()
+    kl = pltpu.make_async_copy(k_ref.at[:, part(core, kv_half)], kv.at[here, first], local.at[0])
+    vl = pltpu.make_async_copy(v_ref.at[:, part(core, kv_half)], kv.at[here, second], local.at[1])
+    kl.start()
+    vl.start()
+    kl.wait()
+    vl.wait()
+    ks.wait()
+    vs.wait()
+
+    def send(o):
+        return pltpu.make_async_remote_copy(
+            src_ref=out.at[o - 1],
+            dst_ref=pool_ref.at[pl.ds(pl.multiple_of((qb + me * CAP) * BLOCK, BLOCK), CAP * BLOCK), :],
+            send_sem=blk_sems.at[0, o - 1],
+            recv_sem=blk_sems.at[1, o - 1],
+            device_id={"blk": lax.rem(me + o, shards)},
+            device_id_type=MESH,
+        )
+
+    def pack(o, carry):
+        to = lax.rem(me + o, shards)
+        for s in range(CAP):
+            which = idx_ref[to * CAP + s]
+            block = kv[0:BLOCK, :]
+            for b in range(1, qb):
+                block = jnp.where(which == b, kv[b * BLOCK:(b + 1) * BLOCK, :], block)
+            out[o - 1, s * BLOCK:(s + 1) * BLOCK, :] = block
+        send(o).start()
+        return carry
+
+    lax.fori_loop(1, shards, pack, 0)
+    own = pltpu.make_async_copy(kv, pool_ref.at[pl.ds(0, qb * BLOCK), :], local.at[0])
+    own.start()
+    qs = to_mate(q_ref.at[:, part(mate, half)], qh_ref.at[here, :], mate_sems, 2, mate)
+    ds = to_mate(do_ref.at[:, part(mate, half)], doh_ref.at[here, :], mate_sems, 3, mate)
+    qs.start()
+    ds.start()
+    ql = pltpu.make_async_copy(q_ref.at[:, part(core, half)], qh_ref.at[here, :], local.at[1])
+    dl = pltpu.make_async_copy(do_ref.at[:, part(core, half)], doh_ref.at[here, :], local.at[2])
+    ql.start()
+    dl.start()
+    own.wait()
+    ql.wait()
+    dl.wait()
+    qs.wait()
+    ds.wait()
+
+    def finish(o, carry):
+        send(o).wait()
+        return carry
+
+    lax.fori_loop(1, shards, finish, 0)
+
+
+def bring_call(idx, q, do, k, v, shards, qb, pool_size):
+    rows, width = q.shape
+    kv_width = k.shape[1]
+    heads = jax.ShapeDtypeStruct((2 * rows, width // 2), q.dtype)
     return pl.pallas_call(
-        functools.partial(combine, shards, qb),
-        out_shape=jax.ShapeDtypeStruct((2, qb * BLOCK, width), jnp.bfloat16),
-        grid_spec=pltpu.PrefetchScalarGridSpec(
-            num_scalar_prefetch=2,
-            grid=(2,),
-            in_specs=[
-                pl.BlockSpec((1, qb * BLOCK, width), lambda t, *_: (t, 0, 0)),
-                pl.BlockSpec((shards, 1, CAP * BLOCK, width), lambda t, *_: (0, t, 0, 0)),
-            ],
-            out_specs=pl.BlockSpec((1, qb * BLOCK, width), lambda t, *_: (t, 0, 0)),
+        functools.partial(bring, shards, qb),
+        out_shape=(heads, heads, jax.ShapeDtypeStruct((pool_size * BLOCK, kv_width), k.dtype)),
+        in_specs=[SMEM, ANY, ANY, ANY, ANY],
+        out_specs=(ANY, ANY, ANY),
+        scratch_shapes=[
+            pltpu.VMEM((qb * BLOCK, kv_width), k.dtype),
+            pltpu.VMEM((shards - 1, CAP * BLOCK, kv_width), k.dtype),
+            pltpu.SemaphoreType.DMA((3,)),
+            pltpu.SemaphoreType.DMA((2, 4)),
+            pltpu.SemaphoreType.DMA((2, shards - 1)),
+        ],
+        compiler_params=pltpu.CompilerParams(
+            collective_id=0, has_side_effects=True, vmem_limit_bytes=40 * 1024 * 1024
         ),
-        compiler_params=pltpu.CompilerParams(vmem_limit_bytes=40 * 1024 * 1024),
-        name="combine",
-    )(asked, rank, grads, back)
+        name="bring",
+    )(idx, q, do, k, v)
+
+
+def give(
+    shards, qb, sel_ref, att_ref, dq_ref, grad_ref, atto_ref, dqo_ref, dko_ref, dvo_ref,
+    own, back, total, done, local, mate_sems, blk_sems,
+):
+    me = lax.axis_index("blk")
+    core = lax.axis_index("uly")
+    mate = 1 - core
+    rows, width = atto_ref.shape
+    half, kv_half = width // 2, dko_ref.shape[1] // 2
+    greet(shards, me, mate)
+
+    def send(o):
+        to = lax.rem(me + o, shards)
+        return pltpu.make_async_remote_copy(
+            src_ref=grad_ref.at[:, pl.ds(pl.multiple_of((qb + to * CAP) * BLOCK, BLOCK), CAP * BLOCK), :],
+            dst_ref=back.at[o - 1],
+            send_sem=blk_sems.at[0, o - 1],
+            recv_sem=blk_sems.at[1, o - 1],
+            device_id={"blk": to},
+            device_id_type=MESH,
+        )
+
+    def start(o, carry):
+        send(o).start()
+        return carry
+
+    lax.fori_loop(1, shards, start, 0)
+    mine = pltpu.make_async_copy(grad_ref.at[:, pl.ds(0, qb * BLOCK), :], own, local.at[0])
+    mine.start()
+    there = part(core, half)
+    ats = to_mate(att_ref.at[part(mate, rows), :], atto_ref.at[:, there], mate_sems, 0, mate)
+    dqs = to_mate(dq_ref.at[part(mate, rows), :], dqo_ref.at[:, there], mate_sems, 1, mate)
+    ats.start()
+    dqs.start()
+    atl = pltpu.make_async_copy(att_ref.at[part(core, rows), :], atto_ref.at[:, there], local.at[1])
+    dql = pltpu.make_async_copy(dq_ref.at[part(core, rows), :], dqo_ref.at[:, there], local.at[2])
+    atl.start()
+    dql.start()
+    mine.wait()
+    total[...] = own[...].astype(jnp.float32)
+
+    def add(o, carry):
+        send(o).wait()
+        source = lax.rem(me - o + shards, shards)
+        for l in range(qb):
+            lo = l * BLOCK
+            pick = sel_ref[source * qb + l]
+            for t in range(2):
+                term = total[t, lo:lo + BLOCK, :]
+                for s in range(CAP):
+                    piece = back[o - 1, t, s * BLOCK:(s + 1) * BLOCK, :].astype(jnp.float32)
+                    term = term + jnp.where(pick == s, piece, 0.0)
+                total[t, lo:lo + BLOCK, :] = term
+        return carry
+
+    lax.fori_loop(1, shards, add, 0)
+    done[...] = total[...].astype(done.dtype)
+    kv_there = part(core, kv_half)
+    kvs = []
+    for t, ref in enumerate((dko_ref, dvo_ref)):
+        kvs.append(to_mate(done.at[t, part(mate, rows), :], ref.at[:, kv_there], mate_sems, 2 + t, mate))
+        kvs.append(pltpu.make_async_copy(done.at[t, part(core, rows), :], ref.at[:, kv_there], local.at[3 + t]))
+    for copy in kvs:
+        copy.start()
+    ats.wait()
+    dqs.wait()
+    atl.wait()
+    dql.wait()
+    for copy in kvs:
+        copy.wait()
+
+
+def give_call(sel, att, dq, grads, shards, qb):
+    tokens, half = att.shape
+    rows, kv_half = tokens // 2, grads.shape[2]
+    wide = jax.ShapeDtypeStruct((rows, 2 * half), att.dtype)
+    narrow = jax.ShapeDtypeStruct((rows, 2 * kv_half), att.dtype)
+    return pl.pallas_call(
+        functools.partial(give, shards, qb),
+        out_shape=(wide, wide, narrow, narrow),
+        in_specs=[SMEM, ANY, ANY, ANY],
+        out_specs=(ANY, ANY, ANY, ANY),
+        scratch_shapes=[
+            pltpu.VMEM((2, qb * BLOCK, kv_half), jnp.bfloat16),
+            pltpu.VMEM((shards - 1, 2, CAP * BLOCK, kv_half), jnp.bfloat16),
+            pltpu.VMEM((2, qb * BLOCK, kv_half), jnp.float32),
+            pltpu.VMEM((2, qb * BLOCK, kv_half), jnp.bfloat16),
+            pltpu.SemaphoreType.DMA((5,)),
+            pltpu.SemaphoreType.DMA((2, 4)),
+            pltpu.SemaphoreType.DMA((2, shards - 1)),
+        ],
+        compiler_params=pltpu.CompilerParams(
+            collective_id=1, has_side_effects=True, vmem_limit_bytes=40 * 1024 * 1024
+        ),
+        name="give",
+    )(sel, att, dq, grads)
 
 
 def plan(pattern, position, shards, qb):
@@ -140,27 +331,24 @@
     pool = jnp.where(mine // qb == position, mine % qb, qb + (mine // qb) * CAP + rank)
     others = jnp.arange(shards, dtype=jnp.int32)[:, None] != position
     asked = lax.dynamic_slice_in_dim(listed, position * qb, qb, 1) * others
-    asked_rank = jnp.where(asked > 0, lax.dynamic_slice_in_dim(rank_all, position * qb, qb, 1), 0)
-    return mine, pool, asked.reshape(-1), asked_rank.reshape(-1)
+    asked_rank = lax.dynamic_slice_in_dim(rank_all, position * qb, qb, 1)
+    pick = jnp.where(asked > 0, asked_rank, -1)
+    slots = jnp.arange(CAP, dtype=jnp.int32)
+    within = jnp.arange(qb, dtype=jnp.int32)
+    idx = jnp.sum(jnp.where(pick[:, None, :] == slots[None, :, None], within, 0), axis=2)
+    return pool, idx.reshape(-1), pick.reshape(-1)
 
 
 def on_device(queries, key_states, value_states, out_grad, pattern):
     shards = lax.axis_size("blk")
     position = lax.axis_index("blk")
-    swap = functools.partial(lax.all_to_all, axis_name="uly", split_axis=1, concat_axis=0, tiled=True)
-    unswap = functools.partial(lax.all_to_all, axis_name="uly", split_axis=0, concat_axis=1, tiled=True)
-    k, v = swap(key_states), swap(value_states)
-    everything = lax.all_gather(jnp.concatenate([k, v], axis=1), "blk", axis=0, tiled=True)
-    q, do = swap(queries), swap(out_grad)
-    qb = q.shape[0] // BLOCK
+    qb = 2 * queries.shape[0] // BLOCK
     kb = pattern.shape[1]
-    rows, pool, asked, rank = plan(pattern, position, shards, qb)
-    att, dq, grads = attend_call(rows, pool, q, do, everything, qb, kb, qb + shards * CAP)
-    width = grads.shape[-1]
-    sent = grads[:, qb * BLOCK:].reshape(2, shards, CAP * BLOCK, width).transpose(1, 0, 2, 3)
-    back = lax.all_to_all(sent, "blk", split_axis=0, concat_axis=0, tiled=True)
-    kv_grad = combine_call(asked, rank, grads, back, qb)
-    return unswap(att), unswap(dq), unswap(kv_grad[0]), unswap(kv_grad[1])
+    pool_size = qb + shards * CAP
+    pool, idx, pick = plan(pattern, position, shards, qb)
+    q, do, kv = bring_call(idx, queries, out_grad, key_states, value_states, shards, qb, pool_size)
+    att, dq, grads = attend_call(pool, pool, q, do, kv, qb, kb, pool_size)
+    return give_call(pick, att, dq, grads, shards, qb)
 
 
 def solution(mesh):

time: 206 us -> 133 us (0.65)
  the two profiles are of different devices: /device:TPU:0 before, /device:TPU:29 now
where the time goes in v1:
time: 133 us
  Pallas kernels  123 us (92%)
  local copies, waits for them, and re-layouts  8.87 us (7%)
    pallas_call x1, Pallas kernels, give_call(): pl.pallas_call(functools.partial(give, shards, qb), out_shape=(wide, wide...  52.4 us
    pallas_call x1, Pallas kernels, bring_call(): pl.pallas_call(functools.partial(bring, shards, qb), out_shape=(heads, he...  52 us
    pallas_call x1, Pallas kernels, attend_call(): pl.pallas_call(functools.partial(attend, cols // HD, qb, kb), out_shape=(...  18.1 us
    unnamed x13, local copies, waits for them, and re-layouts  8.46 us

profile of v1, /device:TPU:29, one launch (start us, length us, event | category | flops | bytes accessed | tf_op | source)
XLA Modules:
  0.0 132.8 jit_solution(9145598554333723298)
XLA Ops:
  0.7 0.1 fusion.2
  0.7 0.8 copy.10
  1.5 0.1 eq.64
  1.6 0.1 fusion
  1.7 0.1 multiply_reduce_fusion
  1.8 0.1 dynamic-slice_select_fusion
  1.9 0.2 select_reduce_fusion
  2.1 0.1 reshape.98.sel_ref
  2.2 0.1 copy.11
  2.3 0.1 copy.12
  2.4 0.1 reshape.100.idx_ref
  2.5 0.0 copy-start
  2.5 1.2 copy-done
  3.7 0.0 copy-start.1
  3.7 1.2 copy-done.1
  4.9 0.0 copy-start.2
  4.9 0.9 copy-done.2
  5.9 0.0 copy-start.3
  5.9 0.9 copy-done.3
  6.8 52.0 %bring.1 = (bf16[256,2048]{1,0:T(8,128)(2,1)S(1)}, bf16[256,2048]{1,0:T(8,128)(2,1)S(1)}, bf16[1280,1024]{1,0:T(8,128)(2,1)S(1)}) custom-call(s32[16]{0:T(128)S(1)} %reshape.100.idx_ref, bf16[128,4096]{1,0:T(8,128)(2,1)S(1)} %copy-done, bf16[128,4096]{1,0:T(8,128)(2,1)S(1)} %copy-done.1, bf16[128,1024]{1,0:T(8,128)(2,1)S(1)} %copy-done.2, ...), custom_call_target="tpu_custom_call" | custom-call | tf_op jit(solution)/shard_map/bring/pallas_call | solution.py:203
  58.9 18.1 %attend.1 = (bf16[256,2048]{1,0:T(8,128)(2,1)S(1)}, bf16[256,2048]{1,0:T(8,128)(2,1)S(1)}, bf16[2,1280,512]{2,1,0:T(8,128)(2,1)S(1)}) custom-call(s32[32]{0:T(128)S(1)} %compare_select_fusion.rows_ref.pool_ref, s32[32]{0:T(128)S(1)} %compare_select_fusion.rows_ref.pool_ref, bf16[256,2048]{1,0:T(8,128)(2,1)S(1)} %get-tuple-element.10.q_ref, ...), custom_call_target="tpu_custom_call" | custom-call | tf_op jit(solution)/shard_map/attend/pallas_call | solution.py:69
  77.0 52.4 %give.1 = (bf16[128,4096]{1,0:T(8,128)(2,1)S(1)}, bf16[128,4096]{1,0:T(8,128)(2,1)S(1)}, bf16[128,1024]{1,0:T(8,128)(2,1)S(1)}, bf16[128,1024]{1,0:T(8,128)(2,1)S(1)}) custom-call(s32[32]{0:T(128)S(1)} %reshape.98.sel_ref, bf16[256,2048]{1,0:T(8,128)(2,1)S(1)} %get-tuple-element.13.att_ref, bf16[256,2048]{1,0:T(8,128)(2,1)S(1)} %get-tuple-element.14.dq_ref, ...), custom_call_target="tpu_custom_call" | custom-call | tf_op jit(solution)/shard_map/give/pallas_call | solution.py:299
  129.4 1.0 copy.17
  130.4 1.0 copy.18
  131.4 0.7 copy.19
  132.1 0.7 copy.20
  (6 shorter events, 0.1 us)
Async XLA Ops:
  2.5 1.2 copy-start
  3.7 1.2 copy-start.1
  4.9 0.9 copy-start.2
  5.9 0.9 copy-start.3

commit v2 on v1

--- a/solution.py
+++ b/solution.py
@@ -127,7 +127,7 @@
 
 def bring(
     shards, qb, idx_ref, q_ref, do_ref, k_ref, v_ref, qh_ref, doh_ref, pool_ref,
-    kv, out, local, mate_sems, blk_sems,
+    kv, far, out, local, mate_sems, twin_sems, blk_sems,
 ):
     me = lax.axis_index("blk")
     core = lax.axis_index("uly")
@@ -151,28 +151,54 @@
     ks.wait()
     vs.wait()
 
-    def send(o):
+    half_size = shards // 2
+    base = me // half_size * half_size
+    place = lax.rem(me, half_size)
+    twin = lax.rem(me + half_size, shards)
+    halves = (first, second)
+
+    def relay(t):
         return pltpu.make_async_remote_copy(
-            src_ref=out.at[o - 1],
-            dst_ref=pool_ref.at[pl.ds(pl.multiple_of((qb + me * CAP) * BLOCK, BLOCK), CAP * BLOCK), :],
-            send_sem=blk_sems.at[0, o - 1],
-            recv_sem=blk_sems.at[1, o - 1],
-            device_id={"blk": lax.rem(me + o, shards)},
+            src_ref=kv.at[:, halves[t]],
+            dst_ref=far.at[:, halves[t]],
+            send_sem=twin_sems.at[0, t],
+            recv_sem=twin_sems.at[1, t],
+            device_id={"blk": twin},
             device_id_type=MESH,
         )
 
-    def pack(o, carry):
-        to = lax.rem(me + o, shards)
+    def send(f, t, o):
+        owner = twin if f else me
+        return pltpu.make_async_remote_copy(
+            src_ref=out.at[f, o, :, halves[t]],
+            dst_ref=pool_ref.at[
+                pl.ds(pl.multiple_of((qb + owner * CAP) * BLOCK, BLOCK), CAP * BLOCK), halves[t]
+            ],
+            send_sem=blk_sems.at[0, f, t, o],
+            recv_sem=blk_sems.at[1, f, t, o],
+            device_id={"blk": base + lax.rem(place + o, half_size)},
+            device_id_type=MESH,
+        )
+
+    def pack(source, f, t, o):
+        to = base + lax.rem(place + o, half_size)
         for s in range(CAP):
-            which = idx_ref[to * CAP + s]
-            block = kv[0:BLOCK, :]
+            which = idx_ref[(f * shards + to) * CAP + s]
+            block = source[0:BLOCK, halves[t]]
             for b in range(1, qb):
-                block = jnp.where(which == b, kv[b * BLOCK:(b + 1) * BLOCK, :], block)
-            out[o - 1, s * BLOCK:(s + 1) * BLOCK, :] = block
-        send(o).start()
+                block = jnp.where(which == b, source[b * BLOCK:(b + 1) * BLOCK, halves[t]], block)
+            out[f, o, s * BLOCK:(s + 1) * BLOCK, halves[t]] = block
+
+    relay(0).start()
+    relay(1).start()
+
+    def near(o, carry):
+        for t in range(2):
+            pack(kv, 0, t, o)
+            send(0, t, o).start()
         return carry
 
-    lax.fori_loop(1, shards, pack, 0)
+    lax.fori_loop(1, half_size, near, 0)
     own = pltpu.make_async_copy(kv, pool_ref.at[pl.ds(0, qb * BLOCK), :], local.at[0])
     own.start()
     qs = to_mate(q_ref.at[:, part(mate, half)], qh_ref.at[here, :], mate_sems, 2, mate)
@@ -183,17 +209,36 @@
     dl = pltpu.make_async_copy(do_ref.at[:, part(core, half)], doh_ref.at[here, :], local.at[2])
     ql.start()
     dl.start()
+    for t in range(2):
+        relay(t).wait()
+
+        def onward(o, carry):
+            pack(far, 1, t, o)
+            send(1, t, o).start()
+            return carry
+
+        lax.fori_loop(1, half_size, onward, 0)
+        pack(far, 1, t, 0)
+    kept = pltpu.make_async_copy(
+        out.at[1, 0],
+        pool_ref.at[pl.ds(pl.multiple_of((qb + twin * CAP) * BLOCK, BLOCK), CAP * BLOCK), :],
+        local.at[3],
+    )
+    kept.start()
     own.wait()
     ql.wait()
     dl.wait()
     qs.wait()
     ds.wait()
+    kept.wait()
 
     def finish(o, carry):
-        send(o).wait()
+        for f in range(2):
+            for t in range(2):
+                send(f, t, o).wait()
         return carry
 
-    lax.fori_loop(1, shards, finish, 0)
+    lax.fori_loop(1, half_size, finish, 0)
 
 
 def bring_call(idx, q, do, k, v, shards, qb, pool_size):
@@ -207,13 +252,15 @@
         out_specs=(ANY, ANY, ANY),
         scratch_shapes=[
             pltpu.VMEM((qb * BLOCK, kv_width), k.dtype),
-            pltpu.VMEM((shards - 1, CAP * BLOCK, kv_width), k.dtype),
-            pltpu.SemaphoreType.DMA((3,)),
+            pltpu.VMEM((qb * BLOCK, kv_width), k.dtype),
+            pltpu.VMEM((2, shards // 2, CAP * BLOCK, kv_width), k.dtype),
+            pltpu.SemaphoreType.DMA((4,)),
             pltpu.SemaphoreType.DMA((2, 4)),
-            pltpu.SemaphoreType.DMA((2, shards - 1)),
+            pltpu.SemaphoreType.DMA((2, 2)),
+            pltpu.SemaphoreType.DMA((2, 2, 2, shards // 2)),
         ],
         compiler_params=pltpu.CompilerParams(
-            collective_id=0, has_side_effects=True, vmem_limit_bytes=40 * 1024 * 1024
+            collective_id=0, has_side_effects=True, vmem_limit_bytes=56 * 1024 * 1024
         ),
         name="bring",
     )(idx, q, do, k, v)
@@ -329,14 +376,18 @@
     my_rank = lax.dynamic_slice_in_dim(rank_all, position, 1, 0)
     rank = jnp.sum(jnp.where(mine[:, None] == ids[None, :], my_rank, 0), axis=1)
     pool = jnp.where(mine // qb == position, mine % qb, qb + (mine // qb) * CAP + rank)
-    others = jnp.arange(shards, dtype=jnp.int32)[:, None] != position
-    asked = lax.dynamic_slice_in_dim(listed, position * qb, qb, 1) * others
-    asked_rank = lax.dynamic_slice_in_dim(rank_all, position * qb, qb, 1)
-    pick = jnp.where(asked > 0, asked_rank, -1)
+    ranked = jnp.where(listed > 0, rank_all, -1)
     slots = jnp.arange(CAP, dtype=jnp.int32)
     within = jnp.arange(qb, dtype=jnp.int32)
-    idx = jnp.sum(jnp.where(pick[:, None, :] == slots[None, :, None], within, 0), axis=2)
-    return pool, idx.reshape(-1), pick.reshape(-1)
+
+    def table(owner_at):
+        pick = lax.dynamic_slice_in_dim(ranked, owner_at * qb, qb, 1)
+        idx = jnp.sum(jnp.where(pick[:, None, :] == slots[None, :, None], within, 0), axis=2)
+        return pick, idx.reshape(-1)
+
+    pick, near = table(position)
+    far = table((position + shards // 2) % shards)[1]
+    return pool, jnp.concatenate([near, far]), pick.reshape(-1)
 
 
 def on_device(queries, key_states, value_states, out_grad, pattern):

time: 133 us -> 123 us (0.925)
  Pallas kernels: 123 us -> 112 us
    pallas_call x1, Pallas kernels: 52 us -> 41.6 us  [bring_call(): pl.pallas_call(functools.partial(bring, shards, qb), out_shape=(heads, he...]
    unnamed x13 -> x11, local copies, waits for them, and re-layouts: 8.46 us -> 8.29 us
where the time goes in v2:
time: 123 us
  Pallas kernels  112 us (91%)
  local copies, waits for them, and re-layouts  9.02 us (7%)
    pallas_call x1, Pallas kernels, give_call(): pl.pallas_call(functools.partial(give, shards, qb), out_shape=(wide, wide...  52.4 us
    pallas_call x1, Pallas kernels, bring_call(): pl.pallas_call(functools.partial(bring, shards, qb), out_shape=(heads, he...  41.6 us
    pallas_call x1, Pallas kernels, attend_call(): pl.pallas_call(functools.partial(attend, cols // HD, qb, kb), out_shape=(...  18.1 us
    unnamed x11, local copies, waits for them, and re-layouts  8.29 us

profile of v2, /device:TPU:29, one launch (start us, length us, event | category | flops | bytes accessed | tf_op | source)
XLA Modules:
  0.0 123.1 jit_solution(15785866483186675343)
XLA Ops:
  0.7 0.1 fusion.2
  0.7 0.8 copy.10
  1.5 0.1 eq.79
  1.6 0.1 fusion
  1.7 0.1 multiply_reduce_fusion
  1.9 0.2 select_reduce_fusion
  2.0 0.1 constant_dynamic-slice_fusion
  2.1 0.1 copy.13
  2.2 0.1 reshape.95.sel_ref
  2.3 0.1 copy.11
  2.4 0.1 copy.12
  2.5 0.1 reshape.97
  2.6 0.1 copy.14
  2.6 0.1 reshape.98
  2.7 0.6 compare_select_fusion.1
  3.3 41.6 %bring.1 = (bf16[256,2048]{1,0:T(8,128)(2,1)}, bf16[256,2048]{1,0:T(8,128)(2,1)}, bf16[1280,1024]{1,0:T(8,128)(2,1)}) custom-call(s32[32]{0:T(128)} %get-tuple-element.19.idx_ref, bf16[128,4096]{1,0:T(8,128)(2,1)} %q_ref.1, bf16[128,4096]{1,0:T(8,128)(2,1)} %do_ref.1, bf16[128,1024]{1,0:T(8,128)(2,1)} %k_ref.1, bf16[128,1024]{1,0:T(8,128)(2,1)} %v_ref.1), custom_call_target="tpu_custom_call" | custom-call | tf_op jit(solution)/shard_map/bring/pallas_call | solution.py:248
  45.0 0.0 copy-start
  45.0 1.7 %copy-done = bf16[1280,1024]{1,0:T(8,128)(2,1)S(1)} copy-done((bf16[1280,1024]{1,0:T(8,128)(2,1)S(1)}, bf16[1280,1024]{1,0:T(8,128)(2,1)}, u32[]{:S(2)}) %copy-start) | copy-done | bytes 2621464
  46.7 0.0 copy-start.1
  46.7 1.2 copy-done.1
  47.9 0.0 copy-start.2
  47.9 1.2 copy-done.2
  49.2 18.1 %attend.1 = (bf16[256,2048]{1,0:T(8,128)(2,1)S(1)}, bf16[256,2048]{1,0:T(8,128)(2,1)S(1)}, bf16[2,1280,512]{2,1,0:T(8,128)(2,1)S(1)}) custom-call(s32[32]{0:T(128)S(1)} %get-tuple-element.18.rows_ref.pool_ref, s32[32]{0:T(128)S(1)} %get-tuple-element.18.rows_ref.pool_ref, bf16[256,2048]{1,0:T(8,128)(2,1)S(1)} %copy-done.1, bf16[256,2048]{1,0:T(8,128)(2,1)S(1)} %copy-done.2, ...), custom_call_target="tpu_custom_call" | custom-call | tf_op jit(solution)/shard_map/attend/pallas_call | solution.py:69
  67.3 52.4 %give.1 = (bf16[128,4096]{1,0:T(8,128)(2,1)S(1)}, bf16[128,4096]{1,0:T(8,128)(2,1)S(1)}, bf16[128,1024]{1,0:T(8,128)(2,1)S(1)}, bf16[128,1024]{1,0:T(8,128)(2,1)S(1)}) custom-call(s32[32]{0:T(128)S(1)} %reshape.95.sel_ref, bf16[256,2048]{1,0:T(8,128)(2,1)S(1)} %get-tuple-element.13.att_ref, bf16[256,2048]{1,0:T(8,128)(2,1)S(1)} %get-tuple-element.14.dq_ref, ...), custom_call_target="tpu_custom_call" | custom-call | tf_op jit(solution)/shard_map/give/pallas_call | solution.py:346
  119.7 1.0 copy.19
  120.7 1.0 copy.20
  121.7 0.7 copy.21
  122.4 0.7 copy.22
  (7 shorter events, 0.1 us)
Async XLA Ops:
  45.0 1.7 %copy-start = (bf16[1280,1024]{1,0:T(8,128)(2,1)S(1)}, bf16[1280,1024]{1,0:T(8,128)(2,1)}, u32[]{:S(2)}) copy-start(bf16[1280,1024]{1,0:T(8,128)(2,1)} %get-tuple-element.12.k_ref.v_ref) | copy-start | bytes 7864324
  46.7 1.2 copy-start.1
  47.9 1.2 copy-start.2

commit v3 on v2

--- a/solution.py
+++ b/solution.py
@@ -90,7 +90,7 @@
                 pltpu.VMEM((pr, HD), jnp.float32),
             ],
         ),
-        compiler_params=pltpu.CompilerParams(vmem_limit_bytes=40 * 1024 * 1024),
+        compiler_params=pltpu.CompilerParams(vmem_limit_bytes=56 * 1024 * 1024),
         name="attend",
     )(rows, pool, q, do, kv, kv)
 
@@ -268,7 +268,7 @@
 
 def give(
     shards, qb, sel_ref, att_ref, dq_ref, grad_ref, atto_ref, dqo_ref, dko_ref, dvo_ref,
-    own, back, total, done, local, mate_sems, blk_sems,
+    own, back, total, fold, low, relayed, done, local, mate_sems, twin_sems, blk_sems,
 ):
     me = lax.axis_index("blk")
     core = lax.axis_index("uly")
@@ -277,22 +277,49 @@
     half, kv_half = width // 2, dko_ref.shape[1] // 2
     greet(shards, me, mate)
 
-    def send(o):
-        to = lax.rem(me + o, shards)
+    half_size = shards // 2
+    base = me // half_size * half_size
+    place = lax.rem(me, half_size)
+    twin = lax.rem(me + half_size, shards)
+
+    def slots_of(owner):
+        return pl.ds(pl.multiple_of((qb + owner * CAP) * BLOCK, BLOCK), CAP * BLOCK)
+
+    def send(f, t, o):
+        member = base + lax.rem(place + o, half_size)
+        owner = lax.rem(member + half_size, shards) if f else member
         return pltpu.make_async_remote_copy(
-            src_ref=grad_ref.at[:, pl.ds(pl.multiple_of((qb + to * CAP) * BLOCK, BLOCK), CAP * BLOCK), :],
-            dst_ref=back.at[o - 1],
-            send_sem=blk_sems.at[0, o - 1],
-            recv_sem=blk_sems.at[1, o - 1],
-            device_id={"blk": to},
+            src_ref=grad_ref.at[t, slots_of(owner), :],
+            dst_ref=back.at[f, t, o],
+            send_sem=blk_sems.at[0, f, t, o],
+            recv_sem=blk_sems.at[1, f, t, o],
+            device_id={"blk": member},
             device_id_type=MESH,
         )
 
-    def start(o, carry):
-        send(o).start()
-        return carry
-
-    lax.fori_loop(1, shards, start, 0)
+    def across(t):
+        return pltpu.make_async_remote_copy(
+            src_ref=low.at[t],
+            dst_ref=relayed.at[t],
+            send_sem=twin_sems.at[0, t],
+            recv_sem=twin_sems.at[1, t],
+            device_id={"blk": twin},
+            device_id_type=MESH,
+        )
+
+    for f, t in ((1, 0), (1, 1), (0, 0), (0, 1)):
+
+        def start(o, carry, f=f, t=t):
+            send(f, t, o).start()
+            return carry
+
+        lax.fori_loop(1, half_size, start, 0)
+    kept = [
+        pltpu.make_async_copy(grad_ref.at[t, slots_of(twin), :], back.at[1, t, 0], local.at[5 + t])
+        for t in range(2)
+    ]
+    kept[0].start()
+    kept[1].start()
     mine = pltpu.make_async_copy(grad_ref.at[:, pl.ds(0, qb * BLOCK), :], own, local.at[0])
     mine.start()
     there = part(core, half)
@@ -304,32 +331,50 @@
     dql = pltpu.make_async_copy(dq_ref.at[part(core, rows), :], dqo_ref.at[:, there], local.at[2])
     atl.start()
     dql.start()
+    fold[...] = jnp.zeros_like(fold)
+
+    def add(into, f, t, o):
+        source = base + lax.rem(place - o + half_size, half_size)
+        for l in range(qb):
+            lo = l * BLOCK
+            pick = sel_ref[(f * shards + source) * qb + l]
+            term = into[t, lo:lo + BLOCK, :]
+            for s in range(CAP):
+                piece = back[f, t, o, s * BLOCK:(s + 1) * BLOCK, :].astype(jnp.float32)
+                term = term + jnp.where(pick == s, piece, 0.0)
+            into[t, lo:lo + BLOCK, :] = term
+
+    for t in range(2):
+        kept[t].wait()
+        add(fold, 1, t, 0)
+
+        def gather(o, carry, t=t):
+            send(1, t, o).wait()
+            add(fold, 1, t, o)
+            return carry
+
+        lax.fori_loop(1, half_size, gather, 0)
+        low[t] = fold[t].astype(low.dtype)
+        across(t).start()
     mine.wait()
     total[...] = own[...].astype(jnp.float32)
-
-    def add(o, carry):
-        send(o).wait()
-        source = lax.rem(me - o + shards, shards)
-        for l in range(qb):
-            lo = l * BLOCK
-            pick = sel_ref[source * qb + l]
-            for t in range(2):
-                term = total[t, lo:lo + BLOCK, :]
-                for s in range(CAP):
-                    piece = back[o - 1, t, s * BLOCK:(s + 1) * BLOCK, :].astype(jnp.float32)
-                    term = term + jnp.where(pick == s, piece, 0.0)
-                total[t, lo:lo + BLOCK, :] = term
-        return carry
-
-    lax.fori_loop(1, shards, add, 0)
-    done[...] = total[...].astype(done.dtype)
+    for t in range(2):
+
+        def near(o, carry, t=t):
+            send(0, t, o).wait()
+            add(total, 0, t, o)
+            return carry
+
+        lax.fori_loop(1, half_size, near, 0)
     kv_there = part(core, kv_half)
     kvs = []
     for t, ref in enumerate((dko_ref, dvo_ref)):
+        across(t).wait()
+        done[t] = (total[t] + relayed[t].astype(jnp.float32)).astype(done.dtype)
         kvs.append(to_mate(done.at[t, part(mate, rows), :], ref.at[:, kv_there], mate_sems, 2 + t, mate))
         kvs.append(pltpu.make_async_copy(done.at[t, part(core, rows), :], ref.at[:, kv_there], local.at[3 + t]))
-    for copy in kvs:
-        copy.start()
+        kvs[-2].start()
+        kvs[-1].start()
     ats.wait()
     dqs.wait()
     atl.wait()
@@ -350,12 +395,16 @@
         out_specs=(ANY, ANY, ANY, ANY),
         scratch_shapes=[
             pltpu.VMEM((2, qb * BLOCK, kv_half), jnp.bfloat16),
-            pltpu.VMEM((shards - 1, 2, CAP * BLOCK, kv_half), jnp.bfloat16),
+            pltpu.VMEM((2, 2, shards // 2, CAP * BLOCK, kv_half), jnp.bfloat16),
+            pltpu.VMEM((2, qb * BLOCK, kv_half), jnp.float32),
             pltpu.VMEM((2, qb * BLOCK, kv_half), jnp.float32),
             pltpu.VMEM((2, qb * BLOCK, kv_half), jnp.bfloat16),
-            pltpu.SemaphoreType.DMA((5,)),
+            pltpu.VMEM((2, qb * BLOCK, kv_half), jnp.bfloat16),
+            pltpu.VMEM((2, qb * BLOCK, kv_half), jnp.bfloat16),
+            pltpu.SemaphoreType.DMA((7,)),
             pltpu.SemaphoreType.DMA((2, 4)),
-            pltpu.SemaphoreType.DMA((2, shards - 1)),
+            pltpu.SemaphoreType.DMA((2, 2)),
+            pltpu.SemaphoreType.DMA((2, 2, 2, shards // 2)),
         ],
         compiler_params=pltpu.CompilerParams(
             collective_id=1, has_side_effects=True, vmem_limit_bytes=40 * 1024 * 1024
@@ -386,8 +435,9 @@
         return pick, idx.reshape(-1)
 
     pick, near = table(position)
-    far = table((position + shards // 2) % shards)[1]
-    return pool, jnp.concatenate([near, far]), pick.reshape(-1)
+    far_pick, far = table((position + shards // 2) % shards)
+    pick = jnp.concatenate([pick.reshape(-1), far_pick.reshape(-1)])
+    return pool, jnp.concatenate([near, far]), pick
 
 
 def on_device(queries, key_states, value_states, out_grad, pattern):

time: 123 us -> 116 us (0.943)
  Pallas kernels: 112 us -> 104 us
    pallas_call x1, Pallas kernels: 52.4 us -> 43.5 us  [give_call(): pl.pallas_call(functools.partial(give, shards, qb), out_shape=(wide, wide...]
where the time goes in v3:
time: 116 us; the launch traced here: 115 us
  Pallas kernels  104 us (90%)
  local copies, waits for them, and re-layouts  9.11 us (8%)
  other arithmetic  1.22 us (1%)
    pallas_call x1, Pallas kernels, give_call(): pl.pallas_call(functools.partial(give, shards, qb), out_shape=(wide, wide...  43.5 us
    pallas_call x1, Pallas kernels, bring_call(): pl.pallas_call(functools.partial(bring, shards, qb), out_shape=(heads, he...  41.6 us
    pallas_call x1, Pallas kernels, attend_call(): pl.pallas_call(functools.partial(attend, cols // HD, qb, kb), out_shape=(...  19.1 us
    unnamed x11, local copies, waits for them, and re-layouts  8.3 us

profile of v3, /device:TPU:29, one launch (start us, length us, event | category | flops | bytes accessed | tf_op | source)
XLA Modules:
  0.0 115.2 jit_solution(4214991288847366338)
XLA Ops:
  0.7 0.1 fusion.2
  0.7 0.8 copy.10
  1.5 0.1 eq.79
  1.6 0.1 fusion
  1.7 0.1 multiply_reduce_fusion
  1.9 0.2 select_reduce_fusion
  2.0 0.1 constant_dynamic-slice_fusion.3
  2.1 0.1 reshape.98
  2.2 0.1 copy.11
  2.3 0.1 reshape.99
  2.4 0.1 copy.13
  2.5 0.1 pad_add_fusion.sel_ref
  2.6 0.1 copy.14
  2.6 0.1 reshape.102
  2.7 0.1 copy.12
  2.8 0.1 reshape.101
  2.9 0.6 compare_select_fusion.1
  3.5 41.6 %bring.1 = (bf16[256,2048]{1,0:T(8,128)(2,1)}, bf16[256,2048]{1,0:T(8,128)(2,1)}, bf16[1280,1024]{1,0:T(8,128)(2,1)}) custom-call(s32[32]{0:T(128)} %get-tuple-element.19.idx_ref, bf16[128,4096]{1,0:T(8,128)(2,1)} %q_ref.1, bf16[128,4096]{1,0:T(8,128)(2,1)} %do_ref.1, bf16[128,1024]{1,0:T(8,128)(2,1)} %k_ref.1, bf16[128,1024]{1,0:T(8,128)(2,1)} %v_ref.1), custom_call_target="tpu_custom_call" | custom-call | tf_op jit(solution)/shard_map/bring/pallas_call | solution.py:248
  45.1 19.1 %attend.1 = (bf16[256,2048]{1,0:T(8,128)(2,1)}, bf16[256,2048]{1,0:T(8,128)(2,1)}, bf16[2,1280,512]{2,1,0:T(8,128)(2,1)}) custom-call(s32[32]{0:T(128)} %get-tuple-element.18.rows_ref.pool_ref, s32[32]{0:T(128)} %get-tuple-element.18.rows_ref.pool_ref, bf16[256,2048]{1,0:T(8,128)(2,1)} %get-tuple-element.10.q_ref, ...), custom_call_target="tpu_custom_call" | custom-call | tf_op jit(solution)/shard_map/attend/pallas_call | solution.py:69
  64.2 0.0 copy-start
  64.2 1.7 %copy-done = bf16[2,1280,512]{2,1,0:T(8,128)(2,1)S(1)} copy-done((bf16[2,1280,512]{2,1,0:T(8,128)(2,1)S(1)}, bf16[2,1280,512]{2,1,0:T(8,128)(2,1)}, u32[]{:S(2)}) %copy-start) | copy-done | bytes 2621464
  65.9 0.0 copy-start.1
  65.9 1.2 %copy-done.1 = bf16[256,2048]{1,0:T(8,128)(2,1)S(1)} copy-done((bf16[256,2048]{1,0:T(8,128)(2,1)S(1)}, bf16[256,2048]{1,0:T(8,128)(2,1)}, u32[]{:S(2)}) %copy-start.1) | copy-done | bytes 1048600
  67.1 0.0 copy-start.2
  67.1 1.2 %copy-done.2 = bf16[256,2048]{1,0:T(8,128)(2,1)S(1)} copy-done((bf16[256,2048]{1,0:T(8,128)(2,1)S(1)}, bf16[256,2048]{1,0:T(8,128)(2,1)}, u32[]{:S(2)}) %copy-start.2) | copy-done | bytes 1048600
  68.4 43.5 %give.1 = (bf16[128,4096]{1,0:T(8,128)(2,1)S(1)}, bf16[128,4096]{1,0:T(8,128)(2,1)S(1)}, bf16[128,1024]{1,0:T(8,128)(2,1)S(1)}, bf16[128,1024]{1,0:T(8,128)(2,1)S(1)}) custom-call(s32[64]{0:T(128)S(1)} %pad_add_fusion.sel_ref, bf16[256,2048]{1,0:T(8,128)(2,1)S(1)} %copy-done.1, bf16[256,2048]{1,0:T(8,128)(2,1)S(1)} %copy-done.2, ...), custom_call_target="tpu_custom_call" | custom-call | tf_op jit(solution)/shard_map/give/pallas_call | solution.py:391
  111.9 1.0 copy.19
  112.8 1.0 copy.20
  113.8 0.7 copy.21
  114.5 0.7 copy.22
  (7 shorter events, 0.1 us)
Async XLA Ops:
  64.2 1.7 %copy-start = (bf16[2,1280,512]{2,1,0:T(8,128)(2,1)S(1)}, bf16[2,1280,512]{2,1,0:T(8,128)(2,1)}, u32[]{:S(2)}) copy-start(bf16[2,1280,512]{2,1,0:T(8,128)(2,1)} %get-tuple-element.15.grad_ref) | copy-start | bytes 7864324
  65.9 1.2 %copy-start.1 = (bf16[256,2048]{1,0:T(8,128)(2,1)S(1)}, bf16[256,2048]{1,0:T(8,128)(2,1)}, u32[]{:S(2)}) copy-start(bf16[256,2048]{1,0:T(8,128)(2,1)} %get-tuple-element.13.att_ref) | copy-start | bytes 3145732
  67.1 1.2 %copy-start.2 = (bf16[256,2048]{1,0:T(8,128)(2,1)S(1)}, bf16[256,2048]{1,0:T(8,128)(2,1)}, u32[]{:S(2)}) copy-start(bf16[256,2048]{1,0:T(8,128)(2,1)} %get-tuple-element.14.dq_ref) | copy-start | bytes 3145732

commit v4 on v3

--- a/solution.py
+++ b/solution.py
@@ -407,7 +407,7 @@
             pltpu.SemaphoreType.DMA((2, 2, 2, shards // 2)),
         ],
         compiler_params=pltpu.CompilerParams(
-            collective_id=1, has_side_effects=True, vmem_limit_bytes=40 * 1024 * 1024
+            collective_id=1, has_side_effects=True, vmem_limit_bytes=56 * 1024 * 1024
         ),
         name="give",
     )(sel, att, dq, grads)

time: 116 us -> 115 us (level)
  local copies, waits for them, and re-layouts: 9.11 us -> 6.36 us
    unnamed x11, local copies, waits for them, and re-layouts: 8.3 us -> 5.55 us
where the time goes in v4:
time: 115 us; the launch traced here: 113 us
  Pallas kernels  105 us (91%)
  local copies, waits for them, and re-layouts  6.36 us (6%)
  other arithmetic  1.73 us (2%)
    pallas_call x1, Pallas kernels, give_call(): pl.pallas_call(functools.partial(give, shards, qb), out_shape=(wide, wide...  43.9 us
    pallas_call x1, Pallas kernels, bring_call(): pl.pallas_call(functools.partial(bring, shards, qb), out_shape=(heads, he...  41.6 us
    pallas_call x1, Pallas kernels, attend_call(): pl.pallas_call(functools.partial(attend, cols // HD, qb, kb), out_shape=(...  19 us
    unnamed x11, local copies, waits for them, and re-layouts  5.55 us

profile of v4, /device:TPU:29, one launch (start us, length us, event | category | flops | bytes accessed | tf_op | source)
XLA Modules:
  0.0 113.4 jit_solution(15828329708487334539)
XLA Ops:
  0.7 0.1 fusion.2
  0.7 0.8 copy.10
  1.5 0.1 eq.79
  1.6 0.1 fusion
  1.7 0.1 multiply_reduce_fusion
  1.9 0.2 select_reduce_fusion
  2.0 0.1 constant_dynamic-slice_fusion.3
  2.1 0.1 reshape.98
  2.2 0.1 copy.11
  2.3 0.1 reshape.99
  2.4 0.1 copy.13
  2.5 0.6 pad_add_fusion.sel_ref
  3.1 0.1 copy.14
  3.2 0.1 reshape.102
  3.2 0.1 copy.12
  3.3 0.1 reshape.101
  3.4 0.6 compare_select_fusion.1
  4.0 41.6 %bring.1 = (bf16[256,2048]{1,0:T(8,128)(2,1)}, bf16[256,2048]{1,0:T(8,128)(2,1)}, bf16[1280,1024]{1,0:T(8,128)(2,1)}) custom-call(s32[32]{0:T(128)} %get-tuple-element.19.idx_ref, bf16[128,4096]{1,0:T(8,128)(2,1)} %q_ref.1, bf16[128,4096]{1,0:T(8,128)(2,1)} %do_ref.1, bf16[128,1024]{1,0:T(8,128)(2,1)} %k_ref.1, bf16[128,1024]{1,0:T(8,128)(2,1)} %v_ref.1), custom_call_target="tpu_custom_call" | custom-call | tf_op jit(solution)/shard_map/bring/pallas_call | solution.py:248
  45.6 19.0 %attend.1 = (bf16[256,2048]{1,0:T(8,128)(2,1)}, bf16[256,2048]{1,0:T(8,128)(2,1)}, bf16[2,1280,512]{2,1,0:T(8,128)(2,1)}) custom-call(s32[32]{0:T(128)} %get-tuple-element.18.rows_ref.pool_ref, s32[32]{0:T(128)} %get-tuple-element.18.rows_ref.pool_ref, bf16[256,2048]{1,0:T(8,128)(2,1)} %get-tuple-element.10.q_ref, ...), custom_call_target="tpu_custom_call" | custom-call | tf_op jit(solution)/shard_map/attend/pallas_call | solution.py:69
  64.7 43.9 %give.1 = (bf16[128,4096]{1,0:T(8,128)(2,1)}, bf16[128,4096]{1,0:T(8,128)(2,1)}, bf16[128,1024]{1,0:T(8,128)(2,1)}, bf16[128,1024]{1,0:T(8,128)(2,1)}) custom-call(s32[64]{0:T(128)} %pad_add_fusion.sel_ref, bf16[256,2048]{1,0:T(8,128)(2,1)} %get-tuple-element.13.att_ref, bf16[256,2048]{1,0:T(8,128)(2,1)} %get-tuple-element.14.dq_ref, ...), custom_call_target="tpu_custom_call" | custom-call | tf_op jit(solution)/shard_map/give/pallas_call | solution.py:391
  108.6 0.0 copy-start
  108.6 0.0 copy-start.2
  108.6 0.0 copy-start.1
  108.6 2.4 %copy.19 = bf16[128,4096]{1,0:T(8,128)(2,1)} copy(bf16[128,4096]{1,0:T(8,128)(2,1)} %get-tuple-element.24) | data formatting | bytes 2097152
  111.0 0.0 copy-done
  111.0 1.0 copy.20
  112.0 0.0 copy-done.2
  112.0 0.7 copy.21
  112.7 0.0 copy-done.1
  112.7 0.7 copy.22
  (7 shorter events, 0.1 us)
Async XLA Ops:
  108.6 2.4 %copy-start = (bf16[128,4096]{1,0:T(8,128)(2,1)S(1)}, bf16[128,4096]{1,0:T(8,128)(2,1)}, u32[]{:S(2)}) copy-start(bf16[128,4096]{1,0:T(8,128)(2,1)} %get-tuple-element.25) | copy-start | bytes 3145732
  108.6 3.4 %copy-start.2 = (bf16[128,1024]{1,0:T(8,128)(2,1)S(1)}, bf16[128,1024]{1,0:T(8,128)(2,1)}, u32[]{:S(2)}) copy-start(bf16[128,1024]{1,0:T(8,128)(2,1)} %get-tuple-element.26) | copy-start | bytes 786436
  108.6 4.1 %copy-start.1 = (bf16[128,1024]{1,0:T(8,128)(2,1)S(1)}, bf16[128,1024]{1,0:T(8,128)(2,1)}, u32[]{:S(2)}) copy-start(bf16[128,1024]{1,0:T(8,128)(2,1)} %get-tuple-element.27) | copy-start | bytes 786436
